TPU v7x, 32 devices: a whole 2x2x4 slice. The times are simulated.
32 devices in a mesh: row: 4 (over z), col: 8 (over y, x, core).
Axes of the slice: x: 2, y: 2, z: 4, core: 2. Of those that a mesh axis runs over, the one named last changes fastest.
Arguments:
- feats: bfloat16 [2048, 4096], P('row', 'col'), may hold values from -6 to 6
- prior_factor: bfloat16 [2048, 2048], P('row', 'col'), may hold values from -0.02 to 0.02, as said below
- ridge: float32 [1024], P('col'), may hold values from 0.5 to 2
Outputs:
- factor: float32 [2048, 1024], P('row', 'col')
Inputs may be any that keep to these rules, and one draw needn't show every extreme that they name: `prior_factor`: entries are independent.
All inputs are finite; a program needn't handle non-finite values.
Results may differ from a plain program's by a relative error of at most 0.0003.
Values may be sent and summed in bfloat16 or wider, within the bound.
A program may use at most 128 MiB of HBM per device.

v0:
```python
import jax
import jax.numpy as jnp
from jax import lax
from jax.sharding import PartitionSpec as P

EDGES = 4096
PANEL = 512


def subject_rows(parts, groups, count):
    width = parts.shape[-1]
    return parts.reshape(groups, count, width).transpose(1, 0, 2).reshape(groups * count, width)


def panel_cholesky(block, panel):
    top = jnp.linalg.cholesky(block[:panel, :panel])
    lower_left = jax.scipy.linalg.solve_triangular(top, block[panel:, :panel].T, lower=True).T
    rest = block[panel:, panel:] - jnp.dot(
        lower_left, lower_left.T, precision=lax.Precision.HIGHEST
    )
    bottom = jnp.linalg.cholesky(rest)
    upper = jnp.concatenate([top, jnp.zeros((panel, block.shape[0] - panel), jnp.float32)], axis=1)
    lower = jnp.concatenate([lower_left, bottom], axis=1)
    return jnp.concatenate([upper, lower], axis=0)


def body(feats, prior_factor, ridge):
    groups = lax.axis_size("row")
    lanes = lax.axis_size("col")
    row_pos = lax.axis_index("row")
    col_pos = lax.axis_index("col")
    rows_here = feats.shape[0]
    cols_here = ridge.shape[0]
    total_cols = cols_here * lanes
    leading = total_cols // groups
    col_feats, col_prior = (
        lax.all_gather(feats[:leading], "row", axis=0, tiled=True),
        lax.all_gather(prior_factor[:leading], "row", axis=0, tiled=True),
    )
    col_feats = subject_rows(col_feats, groups, leading)
    col_prior = subject_rows(col_prior, groups, leading)
    gram_part = jnp.dot(feats, col_feats.T, preferred_element_type=jnp.float32)
    update_part = jnp.dot(prior_factor, col_prior.T, preferred_element_type=jnp.float32)
    wide_feats = feats.astype(jnp.float32)
    wide_cols = col_feats.astype(jnp.float32)
    row_sq, col_sq = lax.psum(
        (jnp.sum(wide_feats * wide_feats, axis=1), jnp.sum(wide_cols * wide_cols, axis=1)), "col"
    )
    gram, update = (
        lax.psum_scatter(gram_part, "col", scatter_dimension=1, tiled=True),
        lax.psum_scatter(update_part, "col", scatter_dimension=1, tiled=True),
    )
    col_start = col_pos * cols_here
    own_sq = lax.dynamic_slice_in_dim(col_sq, col_start, cols_here)
    kernel = jnp.exp(-(row_sq[:, None] + own_sq[None, :] - 2.0 * gram) / EDGES)
    subject = lax.broadcasted_iota(jnp.int32, (rows_here, cols_here), 0) * groups + row_pos
    column = lax.broadcasted_iota(jnp.int32, (rows_here, cols_here), 1) + col_start
    system = kernel + jnp.where(subject == column, ridge[None, :], jnp.zeros_like(kernel)) - update
    head = system[:leading]
    blocks = lax.all_gather(head[None], ("row", "col"), axis=0, tiled=True)
    square = (
        blocks.reshape(groups, lanes, leading, cols_here)
        .transpose(2, 0, 1, 3)
        .reshape(total_cols, total_cols)
    )
    diag_factor = panel_cholesky(square, PANEL)
    wide_rows = lax.all_gather(system, "col", axis=1, tiled=True)
    solved = jax.scipy.linalg.solve_triangular(diag_factor, wide_rows.T, lower=True).T
    factor = lax.dynamic_slice_in_dim(solved, col_start, cols_here, 1)
    return factor


def solution(mesh):
    return jax.shard_map(
        body,
        mesh=mesh,
        in_specs=(P("row", "col"), P("row", "col"), P("col")),
        out_specs=P("row", "col"),
        check_vma=False,
    )
```

profile of v0, /device:TPU:0, one launch (start us, length us, event | category | flops | bytes accessed | tf_op | source)
XLA Modules:
  0.0 595.3 jit_solution(6907661394729003374)
XLA Ops:
  10.1 21.4 %all_gather.13 = bf16[1024,256]{1,0:T(8,128)(2,1)S(1)} all-gather(bf16[256,256]{1,0:T(8,128)(2,1)S(1)} %slice.179), channel_id=1, replica_groups=mesh['row'=4,'col'=8] {'row'}, dimensions={0}, use_global_device_ids=true | all-gather | bytes 655360 | tf_op jit(solution)/shard_map/all_gather | solution.py:38
  34.0 9.6 %all-gather.5.cloned.1.call-done = bf16[1024,512]{1,0:T(8,128)(2,1)} async-done(((bf16[256,512]{1,0:T(8,128)(2,1)}), bf16[1024,512]{1,0:T(8,128)(2,1)}) %all-gather.5.cloned.1.call-update) | async-done | bytes 1048592 | tf_op jit(solution)/shard_map/all_gather | solution.py:37
  43.5 2.2 copy.45
  50.2 14.4 %all-reduce.2 = (f32[1024]{0:T(1024)S(1)}, f32[512]{0:T(512)S(1)}) all-reduce(f32[1024]{0:T(1024)S(1)} %reduce_sum.22, f32[512]{0:T(512)S(1)} %multiply_reduce_fusion.1), channel_id=1, replica_groups=mesh['row'=4,'col'=8] {'col'}, use_global_device_ids=true, to_apply=%region_3.0 | all-reduce | flops 1536 | bytes 12288 | tf_op jit(solution)/shard_map/psum | solution.py:46
  64.7 10.5 %reduce-scatter.5.cloned.1.call-done = f32[512,128]{1,0:T(8,128)} async-done(((f32[512,1024]{1,0:T(8,128)}), f32[512,128]{1,0:T(8,128)}) %reduce-scatter.5.cloned.1.call-update) | async-done | bytes 262160 | tf_op jit(solution)/shard_map/reduce_scatter | solution.py:51
  75.2 44.6 %reduce-scatter.3.cloned.1.call-done = f32[512,128]{1,0:T(8,128)} async-done(((f32[512,1024]{1,0:T(8,128)}), f32[512,128]{1,0:T(8,128)}) %reduce-scatter.3.cloned.1.call-update) | async-done | bytes 262160 | tf_op jit(solution)/shard_map/reduce_scatter | solution.py:50
  122.6 61.4 %all-gather.9.cloned.1.call-done = f32[8192,128]{1,0:T(8,128)} async-done(((f32[256,128]{1,0:T(8,128)}), f32[8192,128]{1,0:T(8,128)}) %all-gather.9.cloned.1.call-update) | async-done | bytes 4194320 | tf_op jit(solution)/shard_map/all_gather | solution.py:60
  184.0 4.6 copy.18
  192.0 3.4 slice_bitcast_fusion
  196.4 11.7 %cholesky.286 = f32[128,128]{1,0:T(8,128)S(1)} custom-call(f32[128,128]{1,0:T(8,128)S(1)} %cholesky.426), custom_call_target="Cholesky" | custom-call | tf_op jit(solution)/shard_map/jit(cholesky)/cholesky | solution.py:16
  208.2 9.8 %custom-call.33 = f32[1,128,128]{1,2,0:T(8,128)S(1)} custom-call(f32[1,128,128]{2,1,0:T(8,128)S(1)} %get-tuple-element.93), custom_call_target="InvertDiagBlocksLowerTriangular" | custom-call | tf_op jit(solution)/shard_map/jit(cholesky)/cholesky | solution.py:16
  220.6 12.1 %cholesky.305 = f32[128,128]{1,0:T(8,128)S(1)} custom-call(f32[128,128]{1,0:T(8,128)S(1)} %cholesky.430), custom_call_target="Cholesky" | custom-call | tf_op jit(solution)/shard_map/jit(cholesky)/cholesky | solution.py:16
  232.8 9.8 %custom-call.34 = f32[1,128,128]{1,2,0:T(8,128)S(1)} custom-call(f32[1,128,128]{2,1,0:T(8,128)S(1)} %get-tuple-element.90), custom_call_target="InvertDiagBlocksLowerTriangular" | custom-call | tf_op jit(solution)/shard_map/jit(cholesky)/cholesky | solution.py:16
  244.2 11.7 %cholesky.326 = f32[128,128]{1,0:T(8,128)S(1)} custom-call(f32[128,128]{1,0:T(8,128)S(1)} %cholesky.435), custom_call_target="Cholesky" | custom-call | tf_op jit(solution)/shard_map/jit(cholesky)/cholesky | solution.py:16
  256.6 9.8 %custom-call.35 = f32[1,128,128]{1,2,0:T(8,128)S(1)} custom-call(f32[1,128,128]{2,1,0:T(8,128)S(1)} %get-tuple-element.87), custom_call_target="InvertDiagBlocksLowerTriangular" | custom-call | tf_op jit(solution)/shard_map/jit(cholesky)/cholesky | solution.py:16
  268.1 11.7 %cholesky.343 = f32[128,128]{1,0:T(8,128)S(1)} custom-call(f32[128,128]{1,0:T(8,128)S(1)} %convolution_subtract_fusion.16), custom_call_target="Cholesky" | custom-call | tf_op jit(solution)/shard_map/jit(cholesky)/cholesky | solution.py:16
  285.0 11.7 %while.2 = (s32[]{:T(128)}, f32[512,512]{1,0:T(8,128)}, s32[4,2]{0,1:T(2,128)S(1)}, f32[4,128,128]{2,1,0:T(8,128)S(1)}, s32[]{:T(128)}) while((s32[]{:T(128)}, f32[512,512]{1,0:T(8,128)}, s32[4,2]{0,1:T(2,128)S(1)}, f32[4,128,128]{2,1,0:T(8,128)S(1)}, s32[]{:T(128)}) %tuple.73), condition=%wide.while_cond, body=%wide.while_body.sunk | while | flops 2 | bytes 131189 | solution.py:17
  285.7 2.3 bitcast_dynamic-update-slice_fusion.4
  288.6 2.3 bitcast_dynamic-update-slice_fusion.4
  291.6 2.3 bitcast_dynamic-update-slice_fusion.4
  294.5 2.2 bitcast_dynamic-update-slice_fusion.4
  296.7 39.9 %custom-call.28 = f32[4,128,128]{1,2,0:T(8,128)} custom-call(f32[4,128,128]{2,1,0:T(8,128)S(1)} %get-tuple-element.13), custom_call_target="InvertDiagBlocksLowerTriangular" | custom-call | tf_op jit(solution)/shard_map/jit(_solve_triangular)/triangular_solve | solution.py:17
  348.1 3.2 convolution_subtract_fusion.9
  355.6 3.1 convolution_subtract_fusion
  360.3 11.7 %cholesky.358 = f32[128,128]{1,0:T(8,128)S(1)} custom-call(f32[128,128]{1,0:T(8,128)S(1)} %cholesky.439), custom_call_target="Cholesky" | custom-call | tf_op jit(solution)/shard_map/jit(cholesky)/cholesky | solution.py:21
  372.0 10.2 %custom-call.36 = f32[1,128,128]{1,2,0:T(8,128)S(1)} custom-call(f32[1,128,128]{2,1,0:T(8,128)S(1)} %get-tuple-element.83), custom_call_target="InvertDiagBlocksLowerTriangular" | custom-call | tf_op jit(solution)/shard_map/jit(cholesky)/cholesky | solution.py:21
  383.6 2.1 convolution_subtract_fusion.11
  388.1 11.7 %cholesky.377 = f32[128,128]{1,0:T(8,128)S(1)} custom-call(f32[128,128]{1,0:T(8,128)S(1)} %cholesky.443), custom_call_target="Cholesky" | custom-call | tf_op jit(solution)/shard_map/jit(cholesky)/cholesky | solution.py:21
  401.6 9.8 %custom-call.37 = f32[1,128,128]{1,2,0:T(8,128)S(1)} custom-call(f32[1,128,128]{2,1,0:T(8,128)S(1)} %get-tuple-element.80), custom_call_target="InvertDiagBlocksLowerTriangular" | custom-call | tf_op jit(solution)/shard_map/jit(cholesky)/cholesky | solution.py:21
  413.8 11.9 %cholesky.398 = f32[128,128]{1,0:T(8,128)S(1)} custom-call(f32[128,128]{1,0:T(8,128)S(1)} %cholesky.448), custom_call_target="Cholesky" | custom-call | tf_op jit(solution)/shard_map/jit(cholesky)/cholesky | solution.py:21
  426.4 9.8 %custom-call.38 = f32[1,128,128]{1,2,0:T(8,128)S(1)} custom-call(f32[1,128,128]{2,1,0:T(8,128)S(1)} %get-tuple-element.77), custom_call_target="InvertDiagBlocksLowerTriangular" | custom-call | tf_op jit(solution)/shard_map/jit(cholesky)/cholesky | solution.py:21
  437.6 11.7 %cholesky.415 = f32[128,128]{1,0:T(8,128)S(1)} custom-call(f32[128,128]{1,0:T(8,128)S(1)} %convolution_subtract_fusion.15), custom_call_target="Cholesky" | custom-call | tf_op jit(solution)/shard_map/jit(cholesky)/cholesky | solution.py:21
  452.9 2.4 fusion
  455.2 27.5 %while.3 = (s32[]{:T(128)}, f32[1024,1024]{1,0:T(8,128)}, s32[8,2]{0,1:T(2,128)S(1)}, f32[8,128,128]{2,1,0:T(8,128)}, s32[]{:T(128)}) while((s32[]{:T(128)}, f32[1024,1024]{1,0:T(8,128)}, s32[8,2]{0,1:T(2,128)S(1)}, f32[8,128,128]{2,1,0:T(8,128)}, s32[]{:T(128)}) %tuple.76), condition=%wide.while_cond.1, body=%wide.while_body.1.sunk | while | flops 2 | bytes 132205 | solution.py:68
  455.9 2.8 bitcast_dynamic-update-slice_fusion.5
  459.3 2.8 bitcast_dynamic-update-slice_fusion.5
  462.7 2.8 bitcast_dynamic-update-slice_fusion.5
  466.2 2.8 bitcast_dynamic-update-slice_fusion.5
  469.6 2.8 bitcast_dynamic-update-slice_fusion.5
  473.1 2.8 bitcast_dynamic-update-slice_fusion.5
  476.5 2.8 bitcast_dynamic-update-slice_fusion.5
  480.0 2.8 bitcast_dynamic-update-slice_fusion.5
  482.7 79.6 %custom-call.29 = f32[8,128,128]{1,2,0:T(8,128)S(1)} custom-call(f32[8,128,128]{2,1,0:T(8,128)} %get-tuple-element.21), custom_call_target="InvertDiagBlocksLowerTriangular" | custom-call | tf_op jit(solution)/shard_map/jit(_solve_triangular)/triangular_solve | solution.py:68
  568.4 2.4 convolution_subtract_fusion.8
  571.3 2.8 convolution_subtract_fusion.10
  574.5 3.2 convolution_subtract_fusion.2
  578.2 3.6 convolution_subtract_fusion.7
  582.3 4.3 convolution_subtract_fusion.1
  (154 shorter events, 70.8 us)
Async XLA Ops:
  7.4 24.7 %copy-start.14 = (bf16[512,256]{1,0:T(8,128)(2,1)S(1)}, bf16[512,256]{1,0:T(8,128)(2,1)}, u32[]{:S(2)}) copy-start(bf16[512,256]{1,0:T(8,128)(2,1)} %param.5) | copy-start | bytes 786436
  7.4 36.1 %all-gather.5.cloned.1.call-start = ((), (), s32[]{:S(2)}) async-start(), calls=%async_computation.2 | async-start | bytes 1310720 | tf_op jit(solution)/shard_map/all_gather | solution.py:37
  9.1 66.1 %reduce-scatter.5.cloned.1.call-start = ((), (), s32[]{:S(2)}) async-start(), calls=%async_computation.4 | async-start | bytes 2359296 | tf_op jit(solution)/shard_map/reduce_scatter | solution.py:51
  33.9 85.9 %reduce-scatter.3.cloned.1.call-start = ((), (), s32[]{:S(2)}) async-start(), calls=%async_computation.3 | async-start | bytes 2359296 | tf_op jit(solution)/shard_map/reduce_scatter | solution.py:50
  43.5 2.5 copy-start.3
  48.0 1.2 copy-start.2
  48.0 71.8 %copy-start.15 = (f32[128]{0:T(128)S(1)}, f32[128]{0:T(128)}, u32[]{:S(2)}) copy-start(f32[128]{0:T(128)} %param.6) | copy-start | bytes 1540
  48.0 136.0 %all-gather.9.cloned.1.call-start = ((), (), s32[]{:S(2)}) async-start(), calls=%async_computation.6 | async-start | bytes 4325376 | tf_op jit(solution)/shard_map/all_gather | solution.py:60
  121.1 1.0 copy-start.12
  121.8 440.5 %all-gather.7.cloned.1.call-start = ((), (), s32[]{:S(2)}) async-start(), calls=%async_computation.5 | async-start | bytes 2359296 | tf_op jit(solution)/shard_map/all_gather | solution.py:67
  189.6 1.9 copy-start
  195.4 1.0 copy-start.5
  285.0 53.9 %copy-start.1 = (f32[512,512]{0,1:T(8,128)S(1)}, f32[512,512]{0,1:T(8,128)}, u32[]{:S(2)}) copy-start(f32[512,512]{0,1:T(8,128)} %get-tuple-element.46) | copy-start | bytes 3145732
  347.4 0.7 copy-start.6
  351.4 4.2 copy-start.7
  354.9 0.7 copy-start.10
  359.3 1.0 copy-start.4
  385.6 67.0 %copy-start.8 = (f32[128,512]{0,1:T(8,128)S(1)}, f32[128,512]{0,1:T(8,128)}, u32[]{:S(2)}) copy-start(f32[128,512]{0,1:T(8,128)} %copy.22) | copy-start | bytes 786436
  385.6 67.0 %copy-start.9 = (f32[128,512]{0,1:T(8,128)S(1)}, f32[128,512]{0,1:T(8,128)}, u32[]{:S(2)}) copy-start(f32[128,512]{0,1:T(8,128)} %copy.23) | copy-start | bytes 786436
  385.7 67.0 %copy-start.11 = (f32[128,512]{0,1:T(8,128)S(1)}, f32[128,512]{0,1:T(8,128)}, u32[]{:S(2)}) copy-start(f32[128,512]{0,1:T(8,128)} %copy-done.10) | copy-start | bytes 786436
  562.4 3.7 copy-start.13
Sparse Core Ops, SparseCore 0:
  9.8 33.7 all-gather.4
  122.0 62.0 all-gather.8
  185.9 26.8 all-gather.6
Sparse Core Ops, SparseCore 1:
  34.0 41.2 reduce-scatter.4
  78.7 41.1 reduce-scatter.2
where the time goes:
time: 601 us; the launch traced here: 595 us
  other arithmetic  288 us (48%)
  waiting for transfers between devices  127 us (21%)
  local copies, waits for them, and re-layouts  66.8 us (11%)
  matrix products  57.1 us (10%)
  blocking collectives  35.9 us (6%)
  between operations  20.6 us (3%)
    another operation x3, other arithmetic, body(): jax.scipy.linalg.solve_triangular(diag_factor, wide_rows.T, lower=True)  82 us
    another operation x15, other arithmetic, panel_cholesky(): bottom = jnp.linalg.cholesky(rest)  79.7 us
    another operation x14, other arithmetic, panel_cholesky(): top = jnp.linalg.cholesky(block[:panel, :panel])  78.9 us
    all_gather x1, waiting for transfers between devices, body(): blocks = lax.all_gather(head[None], ('row', 'col'), axis=0, tiled=True)  61.4 us
    reduce_scatter x1, waiting for transfers between devices, body(): lax.psum_scatter(gram_part, 'col', scatter_dimension=1, tiled=True)  44.6 us
    another operation x3, other arithmetic, panel_cholesky(): jax.scipy.linalg.solve_triangular(top, block[panel:, :panel].T, lower=True)  41.2 us
    another operation x36, local copies, waits for them, and re-layouts  39.1 us
    another operation x15, matrix products, body(): jax.scipy.linalg.solve_triangular(diag_factor, wide_rows.T, lower=True)  24.5 us
  transfers between devices with their start and end apart: 5, of which 4 were waited for; matrix products, arithmetic and copies ran while one was open for 63% of the time, Pallas kernels for 0%

commit v1 on v0

v1 whole, which is shorter than its diff:
```python
import jax
import jax.numpy as jnp
from jax import lax
from jax.sharding import PartitionSpec as P
from jax.experimental import pallas as pl
from jax.experimental.pallas import tpu as pltpu

NB = 128
PB = 16


def split2(x):
    hi = x.astype(jnp.bfloat16)
    lo = (x - hi.astype(jnp.float32)).astype(jnp.bfloat16)
    return hi, lo


def dot3(a, b, b_dim=0):
    ah, al = split2(a)
    bh, bl = split2(b)
    return lax.dot_general(
        jnp.concatenate([ah, ah, al], axis=1),
        jnp.concatenate([bh, bl, bh], axis=b_dim),
        (((1,), (b_dim,)), ((), ())),
        preferred_element_type=jnp.float32,
    )


def spread(row, rows=8):
    return jnp.broadcast_to(row, (rows, row.shape[1]))


def factor_block(block):
    sub = lax.broadcasted_iota(jnp.int32, (8, NB), 0)
    sub2 = lax.broadcasted_iota(jnp.int32, (8, 2 * NB), 0)
    lane = lax.broadcasted_iota(jnp.int32, (NB, NB), 1)
    line = lax.broadcasted_iota(jnp.int32, (NB, NB), 0)
    trail = jnp.concatenate([block, (lane == line).astype(jnp.float32)], axis=1)
    nt = PB // 8
    done = []
    for p in range(NB // PB):
        base = p * PB
        panel = trail[:PB]
        rows = [panel[8 * t:8 * t + 8] for t in range(nt)]
        cols = [
            [
                jnp.broadcast_to(rows[t][:, base + j:base + j + 1], (8, NB)) if t >= j // 8 else None
                for t in range(nt)
            ]
            for j in range(PB)
        ]
        outs = [r for r in rows]
        for j in range(PB):
            tj, ij = divmod(j, 8)
            inv = lax.rsqrt(spread(cols[j][tj][ij:ij + 1]))
            col = [cols[j][t] * inv if t >= tj else None for t in range(nt)]
            prow = spread(rows[tj][ij:ij + 1]) * jnp.concatenate([inv, inv], axis=1)
            outs[tj] = jnp.where(sub2 == ij, prow, outs[tj])
            for k in range(j + 1, PB):
                tk, ik = divmod(k, 8)
                piv = spread(col[tk][ik:ik + 1])
                for t in range(tk, nt):
                    cols[k][t] = cols[k][t] - col[t] * piv
            for t in range(tj, nt):
                rows[t] = rows[t] - jnp.concatenate([col[t], col[t]], axis=1) * prow
        out = jnp.concatenate(outs, axis=0)
        done.append(out)
        if p < NB // PB - 1:
            oh, ol = split2(out)
            rhs = jnp.concatenate([oh, ol, oh], axis=0)
            left = jnp.transpose(out[:, :NB])
            lh, ll = split2(left[base + PB:])
            lhs = jnp.concatenate([lh, lh, ll], axis=1)
            prev = trail[PB:]
            trail = prev - jnp.dot(lhs, rhs, preferred_element_type=jnp.float32)
    full = jnp.concatenate(done, axis=0)
    return jnp.where(lane >= line, full[:, :NB], 0.0), full[:, NB:]


def chol_kernel(col_ref, b_hbm, s_hbm, o_ref, m_ref, t_ref, w_ref, sems):
    n = m_ref.shape[0]
    blocks = n // NB
    own = col_ref[0]
    grp = col_ref[1]
    groups = col_ref.shape[0] - 2
    heads = n // groups
    cb = pltpu.make_async_copy(b_hbm, m_ref, sems.at[0])
    cs = pltpu.make_async_copy(s_hbm, t_ref, sems.at[1])
    cb.start()
    cs.start()
    cb.wait()
    cs.wait()

    def step(k, carry):
        at = pl.ds(pl.multiple_of(k * NB, NB), NB)
        u, w = factor_block(m_ref[at, at])
        new = dot3(w, m_ref[at, :])
        m_ref[at, :] = new
        m_ref[at, at] = u
        x = dot3(t_ref[:, at], w, 1)
        t_ref[...] = t_ref[...] - dot3(x, new)

        @pl.when(k == own)
        def _():
            o_ref[heads:, :] = x
            line = lax.broadcasted_iota(jnp.int32, (NB, n), 0) + k * NB
            lane = lax.broadcasted_iota(jnp.int32, (NB, n), 1)
            mine = jnp.where(lane >= line, m_ref[at, :], 0.0)
            pick = (
                lax.broadcasted_iota(jnp.int32, (heads, n), 1)
                == lax.broadcasted_iota(jnp.int32, (heads, n), 0) * groups + grp
            ).astype(jnp.bfloat16)
            hi, lo = split2(mine)
            lo2 = (mine - hi.astype(jnp.float32) - lo.astype(jnp.float32)).astype(jnp.bfloat16)
            nt = (((1,), (1,)), ((), ()))
            o_ref[:heads, :] = sum(
                lax.dot_general(pick, v, nt, preferred_element_type=jnp.float32) for v in (hi, lo, lo2)
            )

        def update(j, c):
            aj = pl.ds(pl.multiple_of(j * NB, NB), NB)
            m_ref[aj, :] = m_ref[aj, :] - dot3(jnp.transpose(m_ref[at, aj]), m_ref[at, :])
            return c

        lax.fori_loop(k + 1, blocks, update, 0)
        return carry

    lax.fori_loop(0, blocks, step, 0)


def chol_solve(square, rest, own, grp, groups):
    n = square.shape[0]
    pos = jnp.stack([own, grp] + [jnp.int32(0)] * groups).astype(jnp.int32)
    return pl.pallas_call(
        chol_kernel,
        out_shape=jax.ShapeDtypeStruct((n // groups + rest.shape[0], NB), jnp.float32),
        in_specs=[
            pl.BlockSpec(memory_space=pltpu.SMEM),
            pl.BlockSpec(memory_space=pl.ANY),
            pl.BlockSpec(memory_space=pl.ANY),
        ],
        out_specs=pl.BlockSpec(memory_space=pltpu.VMEM),
        scratch_shapes=[
            pltpu.VMEM((n, n), jnp.float32),
            pltpu.VMEM(rest.shape, jnp.float32),
            pltpu.VMEM((NB, NB), jnp.float32),
            pltpu.SemaphoreType.DMA((2,)),
        ],
        compiler_params=pltpu.CompilerParams(vmem_limit_bytes=48 * 1024 * 1024),
    )(pos, square, rest)


EDGES = 4096


def subject_rows(parts, groups, count):
    width = parts.shape[-1]
    return parts.reshape(groups, count, width).transpose(1, 0, 2).reshape(groups * count, width)


def dealt(head, tail, lanes):
    width = head.shape[1]
    both = [head.reshape(lanes, -1, width), tail.reshape(lanes, -1, width)]
    return jnp.concatenate(both, axis=1).reshape(-1, width)


def body(feats, prior_factor, ridge):
    groups = lax.axis_size("row")
    lanes = lax.axis_size("col")
    row_pos = lax.axis_index("row")
    col_pos = lax.axis_index("col")
    cols_here = ridge.shape[0]
    total_cols = cols_here * lanes
    leading = total_cols // groups
    share = leading // lanes
    col_feats, col_prior = (
        lax.all_gather(feats[:leading], "row", axis=0, tiled=True),
        lax.all_gather(prior_factor[:leading], "row", axis=0, tiled=True),
    )
    col_feats = subject_rows(col_feats, groups, leading)
    col_prior = subject_rows(col_prior, groups, leading)
    first = row_pos * leading
    rows_feats = dealt(lax.dynamic_slice_in_dim(col_feats, first, leading), feats[leading:], lanes)
    rows_prior = dealt(lax.dynamic_slice_in_dim(col_prior, first, leading), prior_factor[leading:], lanes)
    subject = dealt(
        first + lax.broadcasted_iota(jnp.int32, (leading, 1), 0),
        jnp.full((feats.shape[0] - leading, 1), -1, jnp.int32),
        lanes,
    )
    col_start = col_pos * cols_here
    column = lax.broadcasted_iota(jnp.int32, (1, total_cols), 1)
    own_ridge = lax.dynamic_update_slice(jnp.zeros((total_cols,), jnp.float32), ridge, (col_start,))
    wide_rows = rows_feats.astype(jnp.float32)
    wide_cols = col_feats.astype(jnp.float32)
    gram = jnp.dot(rows_feats, col_feats.T, preferred_element_type=jnp.float32)
    dist = (
        jnp.sum(wide_rows * wide_rows, axis=1)[:, None]
        + jnp.sum(wide_cols * wide_cols, axis=1)[None, :]
        - 2.0 * gram
    )
    update = jnp.dot(rows_prior, col_prior.T, preferred_element_type=jnp.float32)
    update = update - jnp.where(subject == column, own_ridge[None, :], 0.0)
    sums = lax.psum_scatter(
        jnp.concatenate([dist, update], axis=1), "col", scatter_dimension=0, tiled=True
    )
    system = jnp.exp(-sums[:, :total_cols] / EDGES) - sums[:, total_cols:]
    square = lax.all_gather(system[:share], ("row", "col"), axis=0, tiled=True)
    rest = lax.all_gather(system[share:], "col", axis=0, tiled=True)
    out = chol_solve(square, rest, col_start // NB, row_pos, groups)
    if cols_here < NB:
        out = lax.dynamic_slice_in_dim(out, col_start % NB, cols_here, 1)
    return out


def solution(mesh):
    return jax.shard_map(
        body,
        mesh=mesh,
        in_specs=(P("row", "col"), P("row", "col"), P("col")),
        out_specs=P("row", "col"),
        check_vma=False,
    )
```

time: 601 us -> 257 us (0.43)
  other arithmetic: 288 us -> 6.63 us
  matrix products: 57.1 us -> 2.25 us
  local copies, waits for them, and re-layouts: 66.8 us -> 12.2 us
  Pallas kernels: 0 us -> 50.3 us
  waiting for transfers between devices: 127 us -> 150 us
  blocking collectives: 35.9 us -> 21.8 us
  between operations: 20.6 us -> 13.3 us
    another operation x35 -> x1, other arithmetic: 282 us -> 0.08 us  [chol_solve(): pos = jnp.stack([own, grp] + [jnp.int32(0)] * groups).astype(jnp.int32)]
    pallas_call x0 -> x1, Pallas kernels: none -> 50.3 us  [chol_solve(): pl.pallas_call(chol_kernel, out_shape=jax.ShapeDtypeStruct((n // groups +...]
    another operation x34 -> x0, matrix products: 50.1 us -> none  [the longest x15 24.5 us: body(): jax.scipy.linalg.solve_triangular(diag_factor, wide_rows.T, lower=True)]
    another operation x51 -> x1, local copies, waits for them, and re-layouts: 46.4 us -> 0.01 us
    all_gather x2, waiting for transfers between devices: 61.5 us -> 88.3 us  [the longest x1 65.2 us: body(): square = lax.all_gather(system[:share], ('row', 'col'), axis=0, tiled=True)]
    psum x1 -> x0, blocking collectives: 14.4 us -> none  [body(): lax.psum((jnp.sum(wide_feats * wide_feats, axis=1), jnp.sum(wide_cols * w...]
    reduce_scatter x2 -> x1, waiting for transfers between devices: 55.2 us -> 51.1 us  [body(): lax.psum_scatter(jnp.concatenate([dist, update], axis=1), 'col', scatter_...]
  transfers between devices with their start and end apart: 5 -> 4, of which waited for: 4 -> 4; matrix products, arithmetic and copies ran while one was open for 63% -> 1% of each run, Pallas kernels for 0% -> 0%
where the time goes in v1:
time: 257 us
  waiting for transfers between devices  150 us (58%)
  Pallas kernels  50.3 us (20%)
  blocking collectives  21.8 us (8%)
  between operations  13.3 us (5%)
  local copies, waits for them, and re-layouts  12.2 us (5%)
  other arithmetic  6.63 us (3%)
    all_gather x1, waiting for transfers between devices, body(): square = lax.all_gather(system[:share], ('row', 'col'), axis=0, tiled=True)  65.2 us
    reduce_scatter x1, waiting for transfers between devices, body(): lax.psum_scatter(jnp.concatenate([dist, update], axis=1), 'col', scatter_...  51.1 us
    pallas_call x1, Pallas kernels, chol_solve(): pl.pallas_call(chol_kernel, out_shape=jax.ShapeDtypeStruct((n // groups +...  50.3 us
    all_gather x1, waiting for transfers between devices, body(): rest = lax.all_gather(system[share:], 'col', axis=0, tiled=True)  23.1 us
    all_gather x1, blocking collectives, body(): lax.all_gather(prior_factor[:leading], 'row', axis=0, tiled=True)  21.8 us
    all_gather x1, waiting for transfers between devices, body(): lax.all_gather(feats[:leading], 'row', axis=0, tiled=True)  10.2 us
  transfers between devices with their start and end apart: 4, of which 4 were waited for; matrix products, arithmetic and copies ran while one was open for 1% of the time, Pallas kernels for 0%

profile of v1, /device:TPU:0, one launch (start us, length us, event | category | flops | bytes accessed | tf_op | source)
XLA Modules:
  0.0 256.7 jit_solution(291285546548510796)
XLA Ops:
  6.5 0.0 copy-start.3
  6.5 0.0 all-gather.4.cloned.1.call-start
  6.5 1.8 fusion.2
  8.3 0.0 all-gather.4.cloned.1.call-update
  8.3 0.0 reduce-scatter.2.cloned.1.call-start
  8.4 0.1 eq.15
  8.5 1.0 fusion.4
  9.5 21.8 %all_gather.13 = bf16[1024,256]{1,0:T(8,128)(2,1)S(1)} all-gather(bf16[256,256]{1,0:T(8,128)(2,1)S(1)} %get-tuple-element.9), channel_id=1, replica_groups=mesh['row'=4,'col'=8] {'row'}, dimensions={0}, use_global_device_ids=true | all-gather | bytes 655360 | tf_op jit(solution)/shard_map/all_gather | solution.py:178
  31.3 0.4 copy.11
  31.7 0.1 reshape.69
  31.8 0.0 copy-done.3
  31.8 0.2 dynamic_update_slice.5
  32.1 0.5 select_subtract_fusion
  32.6 10.2 %all-gather.4.cloned.1.call-done = bf16[1024,512]{1,0:T(8,128)(2,1)} async-done(((bf16[256,512]{1,0:T(8,128)(2,1)}), bf16[1024,512]{1,0:T(8,128)(2,1)}) %all-gather.4.cloned.1.call-update) | async-done | bytes 1048592 | tf_op jit(solution)/shard_map/all_gather | solution.py:177
  42.8 2.1 multiply_reduce_fusion
  44.9 2.0 copy.10
  46.9 1.1 reshape.64
  48.0 0.0 copy-start.2
  48.0 1.1 constant_dynamic-slice_fusion.1
  49.1 0.2 multiply_reduce_fusion.1
  49.3 0.9 pad_maximum_fusion.1
  50.1 0.1 add.54
  50.3 0.1 add.52
  50.3 0.0 copy-done.2
  50.3 1.8 multiply_subtract_fusion
  52.1 2.3 pad_maximum_fusion
  54.5 0.0 reduce-scatter.2.cloned.1.call-update
  54.5 0.0 all-gather.8.cloned.1.call-start
  54.5 51.1 %reduce-scatter.2.cloned.1.call-done = f32[64,2048]{1,0:T(8,128)} async-done(((f32[512,2048]{1,0:T(8,128)}), f32[64,2048]{1,0:T(8,128)}) %reduce-scatter.2.cloned.1.call-update) | async-done | bytes 524304 | tf_op jit(solution)/shard_map/reduce_scatter | solution.py:203
  105.7 1.1 slice_subtract_fusion
  106.7 0.7 fusion.3
  107.4 0.0 all-gather.8.cloned.1.call-update
  107.5 0.0 all-gather.6.cloned.1.call-start
  107.5 0.5 all-gather.6.cloned.1.call-update
  108.1 0.1 pad_add_fusion.col_ref
  108.1 23.1 %all-gather.8.cloned.1.call-done.s_hbm = f32[256,1024]{1,0:T(8,128)} async-done(((f32[32,1024]{1,0:T(8,128)}), f32[256,1024]{1,0:T(8,128)}) %all-gather.8.cloned.1.call-update) | async-done | bytes 1048592 | tf_op jit(solution)/shard_map/all_gather | solution.py:208
  131.2 65.2 %all-gather.6.cloned.1.call-done.b_hbm = f32[1024,1024]{1,0:T(8,128)} async-done(((f32[32,1024]{1,0:T(8,128)}), f32[1024,1024]{1,0:T(8,128)}) %all-gather.6.cloned.1.call-update) | async-done | bytes 4194320 | tf_op jit(solution)/shard_map/all_gather | solution.py:207
  196.4 0.0 copy-start
  196.4 2.2 copy-done
  198.6 0.0 copy-start.1
  198.6 1.2 copy-done.1
  199.8 50.3 %shard_map.37 = f32[512,128]{1,0:T(8,128)} custom-call(s32[6]{0:T(128)S(1)} %pad_add_fusion.col_ref, f32[1024,1024]{1,0:T(8,128)S(1)} %copy-done, f32[256,1024]{1,0:T(8,128)S(1)} %copy-done.1), custom_call_target="tpu_custom_call" | custom-call | tf_op jit(solution)/shard_map/pallas_call | solution.py:134
  (6 shorter events, 0.0 us)
Async XLA Ops:
  6.5 25.3 %copy-start.3 = (f32[128]{0:T(128)S(1)}, f32[128]{0:T(128)}, u32[]{:S(2)}) copy-start(f32[128]{0:T(128)} %param.5) | copy-start | bytes 1540
  6.5 36.3 %all-gather.4.cloned.1.call-start = ((), (), s32[]{:S(2)}) async-start(), calls=%async_computation.1 | async-start | bytes 1310720 | tf_op jit(solution)/shard_map/all_gather | solution.py:177
  8.3 97.3 %reduce-scatter.2.cloned.1.call-start = ((), (), s32[]{:S(2)}) async-start(), calls=%async_computation.2 | async-start | bytes 4718592 | tf_op jit(solution)/shard_map/reduce_scatter | solution.py:203
  48.0 2.3 copy-start.2
  54.5 76.8 %all-gather.8.cloned.1.call-start = ((), (), s32[]{:S(2)}) async-start(), calls=%async_computation.4 | async-start | bytes 1179648 | tf_op jit(solution)/shard_map/all_gather | solution.py:208
  107.5 89.0 %all-gather.6.cloned.1.call-start = ((), (), s32[]{:S(2)}) async-start(), calls=%async_computation.3 | async-start | bytes 4325376 | tf_op jit(solution)/shard_map/all_gather | solution.py:207
  196.4 2.2 copy-start
  198.6 1.2 copy-start.1
Sparse Core Ops, SparseCore 0:
  8.9 33.8 all-gather.3
  54.6 51.0 reduce-scatter.1
  107.7 23.4 all-gather.7
  134.4 62.0 all-gather.5

commit v2 on v1

--- a/solution.py
+++ b/solution.py
@@ -151,7 +151,146 @@
 
 
 EDGES = 4096
-
+MESH = pl.DeviceIdType.MESH
+
+
+def exchange_kernel(parts_ref, sq_ref, rs_ref, got1, acc, got2, send1, recv1, send2, recv2, sends, arrive):
+    groups, lanes = sq_ref.shape[:2]
+    share, width = sq_ref.shape[2:]
+    i = lax.axis_index("row")
+    c = lax.axis_index("col")
+    core, x, y = lax.rem(c, 2), lax.rem(c // 2, 2), c // 4
+    sib = c + 1 - 2 * core
+    xn = c + 2 - 4 * x
+    yn = c + 4 - 8 * y
+    dg = xn + 4 - 8 * y
+    planes = [lax.rem(i + d, groups) for d in range(groups)]
+    barrier = pltpu.get_barrier_semaphore()
+    for col in (sib, xn, yn, dg):
+        pl.semaphore_signal(barrier, inc=1, device_id=(i, col), device_id_type=MESH)
+    for z in planes[1:]:
+        pl.semaphore_signal(barrier, inc=1, device_id=(z, c), device_id_type=MESH)
+    pl.semaphore_wait(barrier, 3 + groups)
+
+    def remote(src, dst, s, r, target):
+        copy = pltpu.make_async_remote_copy(
+            src_ref=src, dst_ref=dst, send_sem=s, recv_sem=r, device_id=target, device_id_type=MESH
+        )
+        copy.start()
+        return copy
+
+    order = [dg // 2, xn // 2, yn // 2, c // 2]
+    pair = [
+        remote(parts_ref.at[q, 1 - core], got1.at[n], send1.at[n], recv1.at[n], (i, sib))
+        for n, q in enumerate(order)
+    ]
+    across = []
+    for n, q in enumerate(order):
+        pair[n].wait_recv()
+        acc[n] = parts_ref[q, core] + got1[n]
+        if n < 3:
+            across.append(
+                remote(acc.at[n], got2.at[n], send2.at[n], recv2.at[n], (i, (dg, xn, yn)[n]))
+            )
+    for copy in across:
+        copy.wait_recv()
+    total = acc[3] + got2[0] + got2[1] + got2[2]
+    system = jnp.exp(-total[:, :width] / EDGES) - total[:, width:]
+    sq_ref[i, c] = system[:share]
+    rs_ref[c] = system[share:]
+
+    started = []
+
+    def pass_on(z, col, target):
+        n = len(started)
+        started.append(
+            remote(sq_ref.at[z, col], sq_ref.at[z, col], sends.at[n], arrive.at[z * lanes + col], target)
+        )
+
+    def pass_rest(col, target):
+        n = len(started)
+        started.append(
+            remote(rs_ref.at[col], rs_ref.at[col], sends.at[n], arrive.at[groups * lanes + col], target)
+        )
+
+    def await_block(z, col):
+        pltpu.make_async_copy(sq_ref.at[z, col], sq_ref.at[z, col], arrive.at[z * lanes + col]).wait()
+
+    def await_rest(col):
+        pltpu.make_async_copy(rs_ref.at[col], rs_ref.at[col], arrive.at[groups * lanes + col]).wait()
+
+    for z in planes[1:]:
+        pass_on(i, c, (z, c))
+    for z in planes:
+        if z is not planes[0]:
+            await_block(z, c)
+        pass_on(z, c, (i, xn))
+        pass_on(z, c, (i, yn))
+        pass_on(z, c, (i, sib))
+        if z is planes[0]:
+            for col in (xn, yn, sib):
+                pass_rest(c, (i, col))
+    for n, z in enumerate(planes):
+        await_block(z, xn)
+        if n < groups // 2:
+            pass_on(z, xn, (i, yn))
+        pass_on(z, xn, (i, sib))
+        await_block(z, yn)
+        if n >= groups // 2:
+            pass_on(z, yn, (i, xn))
+        pass_on(z, yn, (i, sib))
+        if n == 0:
+            await_rest(xn)
+            pass_rest(xn, (i, yn))
+            pass_rest(xn, (i, sib))
+            await_rest(yn)
+            pass_rest(yn, (i, sib))
+    for n, z in enumerate(planes):
+        await_block(z, dg)
+        pass_on(z, dg, (i, sib))
+        if n == 0:
+            await_rest(dg)
+            pass_rest(dg, (i, sib))
+    other = [sib + d for d in (0, xn - c, yn - c, dg - c)]
+    for col in other:
+        for z in planes:
+            await_block(z, col)
+        await_rest(col)
+    for copy in pair + across + started:
+        copy.wait_send()
+
+
+def exchange(parts, groups, lanes, share):
+    rows, wide = parts.shape
+    each = rows // lanes
+    width = wide // 2
+    f32 = jnp.float32
+    dma = pltpu.SemaphoreType.DMA
+    vmem = pl.BlockSpec(memory_space=pltpu.VMEM)
+    square, rest = pl.pallas_call(
+        exchange_kernel,
+        out_shape=(
+            jax.ShapeDtypeStruct((groups, lanes, share, width), f32),
+            jax.ShapeDtypeStruct((lanes, each - share, width), f32),
+        ),
+        in_specs=[vmem],
+        out_specs=(vmem, vmem),
+        scratch_shapes=[
+            pltpu.VMEM((4, each, wide), f32),
+            pltpu.VMEM((4, each, wide), f32),
+            pltpu.VMEM((3, each, wide), f32),
+            dma((4,)),
+            dma((4,)),
+            dma((3,)),
+            dma((3,)),
+            dma((64,)),
+            dma((groups * lanes + lanes,)),
+        ],
+        compiler_params=pltpu.CompilerParams(
+            collective_id=1, has_side_effects=True, vmem_limit_bytes=40 * 1024 * 1024
+        ),
+    )(parts.reshape(lanes // 2, 2, each, wide))
+    return square.reshape(-1, width), rest.reshape(-1, width)
 
 def subject_rows(parts, groups, count):
     width = parts.shape[-1]
@@ -200,12 +339,16 @@
     )
     update = jnp.dot(rows_prior, col_prior.T, preferred_element_type=jnp.float32)
     update = update - jnp.where(subject == column, own_ridge[None, :], 0.0)
-    sums = lax.psum_scatter(
-        jnp.concatenate([dist, update], axis=1), "col", scatter_dimension=0, tiled=True
-    )
-    system = jnp.exp(-sums[:, :total_cols] / EDGES) - sums[:, total_cols:]
-    square = lax.all_gather(system[:share], ("row", "col"), axis=0, tiled=True)
-    rest = lax.all_gather(system[share:], "col", axis=0, tiled=True)
+    parts = jnp.concatenate([dist, update], axis=1)
+    if (groups, lanes) == (4, 8):
+        square, rest = exchange(parts, groups, lanes, share)
+    else:
+        sums = lax.psum_scatter(
+            parts, "col", scatter_dimension=0, tiled=True
+        )
+        system = jnp.exp(-sums[:, :total_cols] / EDGES) - sums[:, total_cols:]
+        square = lax.all_gather(system[:share], ("row", "col"), axis=0, tiled=True)
+        rest = lax.all_gather(system[share:], "col", axis=0, tiled=True)
     out = chol_solve(square, rest, col_start // NB, row_pos, groups)
     if cols_here < NB:
         out = lax.dynamic_slice_in_dim(out, col_start % NB, cols_here, 1)

time: 257 us -> 172 us (0.67)
  the two profiles are of different devices: /device:TPU:0 before, /device:TPU:11 now
where the time goes in v2:
time: 172 us
  Pallas kernels  114 us (66%)
  blocking collectives  15.2 us (9%)
  waiting for transfers between devices  15.1 us (9%)
  between operations  13.5 us (8%)
  local copies, waits for them, and re-layouts  8.05 us (5%)
  other arithmetic  3.55 us (2%)
  matrix products  2.26 us (1%)
    pallas_call x1, Pallas kernels, exchange(): pl.pallas_call(exchange_kernel, out_shape=(jax.ShapeDtypeStruct((groups,...  63.7 us
    pallas_call x1, Pallas kernels, chol_solve(): pl.pallas_call(chol_kernel, out_shape=jax.ShapeDtypeStruct((n // groups +...  50.3 us
    all_gather x1, blocking collectives, body(): lax.all_gather(prior_factor[:leading], 'row', axis=0, tiled=True)  15.2 us
    all_gather x1, waiting for transfers between devices, body(): lax.all_gather(feats[:leading], 'row', axis=0, tiled=True)  15.1 us
    reshape x4, local copies, waits for them, and re-layouts, subject_rows(): parts.reshape(groups, count, width).transpose(1, 0, 2)  3.69 us
  transfers between devices with their start and end apart: 1, of which 1 were waited for; matrix products, arithmetic and copies ran while one was open for 1% of the time, Pallas kernels for 0%

profile of v2, /device:TPU:11, one launch (start us, length us, event | category | flops | bytes accessed | tf_op | source)
XLA Modules:
  0.0 171.7 jit_solution(642593810505160393)
XLA Ops:
  6.5 0.0 copy-start.1
  6.5 0.0 all-gather.2.cloned.1.call-start
  6.5 1.8 %fusion = (bf16[256,512]{1,0:T(8,128)(2,1)}, bf16[256,512]{1,0:T(8,128)(2,1)S(1)}) fusion(bf16[512,512]{1,0:T(8,128)(2,1)} %param.3), kind=kLoop, calls=%fused_computation.14 | loop fusion | bytes 1048576 | tf_op jit(solution)/shard_map/slice | solution.py:316
  8.3 0.0 all-gather.2.cloned.1.call-update
  8.4 0.1 eq.15
  8.5 1.0 fusion.1
  9.4 15.2 %all_gather.7 = bf16[1024,256]{1,0:T(8,128)(2,1)S(1)} all-gather(bf16[256,256]{1,0:T(8,128)(2,1)S(1)} %get-tuple-element.11), channel_id=1, replica_groups=mesh['row'=4,'col'=8] {'row'}, dimensions={0}, use_global_device_ids=true | all-gather | bytes 655360 | tf_op jit(solution)/shard_map/all_gather | solution.py:317
  24.7 0.4 copy.11
  25.1 0.1 reshape.78
  25.2 0.0 copy-done.1
  25.3 0.2 dynamic_update_slice.5
  25.5 0.1 pad_add_fusion.col_ref
  25.6 0.5 select_subtract_fusion
  26.1 15.1 %all-gather.2.cloned.1.call-done = bf16[1024,512]{1,0:T(8,128)(2,1)} async-done(((bf16[256,512]{1,0:T(8,128)(2,1)}), bf16[1024,512]{1,0:T(8,128)(2,1)}) %all-gather.2.cloned.1.call-update) | async-done | bytes 1048592 | tf_op jit(solution)/shard_map/all_gather | solution.py:316
  41.2 2.1 %multiply_reduce_fusion = f32[256,4]{1,0:T(8,128)S(1)} fusion(bf16[4,256,512]{2,1,0:T(8,128)(2,1)} %bitcast.30), kind=kLoop, calls=%fused_computation.4 | loop fusion | flops 1571840 | bytes 1052672 | tf_op jit(solution)/shard_map/reduce_sum | solution.py:337
  43.3 2.0 %copy.10 = bf16[4,256,512]{2,0,1:T(4,128)(2,1)S(1)} copy(bf16[4,256,512]{2,1,0:T(8,128)(2,1)} %bitcast.31) | data formatting | bytes 2097152 | tf_op jit(solution)/shard_map/reshape | solution.py:297
  45.3 1.1 reshape.73
  46.4 0.0 copy-start
  46.4 1.1 constant_dynamic-slice_fusion.1
  47.5 0.2 multiply_reduce_fusion.1
  47.7 0.8 pad_maximum_fusion.1
  48.5 0.1 add.52
  48.6 0.1 add.50
  48.7 0.0 copy-done
  48.7 1.8 %multiply_subtract_fusion = f32[512,1024]{1,0:T(8,128)S(1)} fusion(bf16[512,512]{1,0:T(8,128)(2,1)} %bitcast.39, bf16[1024,512]{1,0:T(8,128)(2,1)S(1)} %copy-done, f32[1024]{0:T(1024)S(1)} %add.52, f32[512]{0:T(512)S(1)} %add.50), kind=kOutput, calls=%fused_computation.3 | convolution fusion | flops 538443776 | bytes 3676160 | tf_op jit(solution)/shard_map/dot_general | solution.py:334
  50.5 0.4 pad_maximum_fusion
  50.9 63.7 %shard_map.37 = (f32[4,8,32,1024]{3,2,1,0:T(8,128)S(1)}, f32[8,32,1024]{2,1,0:T(8,128)S(1)}) custom-call(f32[4,2,64,2048]{3,2,1,0:T(8,128)S(1)} %bitcast.27), custom_call_target="tpu_custom_call" | custom-call | tf_op jit(solution)/shard_map/pallas_call | solution.py:270
  114.6 50.3 %shard_map.38 = f32[512,128]{1,0:T(8,128)} custom-call(s32[6]{0:T(128)S(1)} %pad_add_fusion.col_ref, f32[1024,1024]{1,0:T(8,128)S(1)} %bitcast.28, f32[256,1024]{1,0:T(8,128)S(1)} %bitcast.29), custom_call_target="tpu_custom_call" | custom-call | tf_op jit(solution)/shard_map/pallas_call | solution.py:134
  (6 shorter events, 0.0 us)
Async XLA Ops:
  6.5 18.7 %copy-start.1 = (f32[128]{0:T(128)S(1)}, f32[128]{0:T(128)}, u32[]{:S(2)}) copy-start(f32[128]{0:T(128)} %param.5) | copy-start | bytes 1540
  6.5 34.7 %all-gather.2.cloned.1.call-start = ((), (), s32[]{:S(2)}) async-start(), calls=%async_computation | async-start | bytes 1310720 | tf_op jit(solution)/shard_map/all_gather | solution.py:316
  46.4 2.3 %copy-start = (bf16[1024,512]{1,0:T(8,128)(2,1)S(1)}, bf16[1024,512]{1,0:T(8,128)(2,1)}, u32[]{:S(2)}) copy-start(bf16[1024,512]{1,0:T(8,128)(2,1)} %reshape.73) | copy-start | bytes 3145732
Sparse Core Ops, SparseCore 0:
  8.9 32.2 all-gather.1

commit v3 on v2

--- a/solution.py
+++ b/solution.py
@@ -1,3 +1,4 @@
+import functools
 import jax
 import jax.numpy as jnp
 from jax import lax
@@ -6,7 +7,9 @@
 from jax.experimental.pallas import tpu as pltpu
 
 NB = 128
-PB = 16
+PB = 32
+TILE = 256
+STOPS = (1, 2)
 
 
 def split2(x):
@@ -77,7 +80,7 @@
     return jnp.where(lane >= line, full[:, :NB], 0.0), full[:, NB:]
 
 
-def chol_kernel(col_ref, b_hbm, s_hbm, o_ref, m_ref, t_ref, w_ref, sems):
+def chol_kernel(col_ref, b_hbm, s_hbm, o_ref, m_ref, t_ref, l_ref, r_ref, x_ref, sems):
     n = m_ref.shape[0]
     blocks = n // NB
     own = col_ref[0]
@@ -91,24 +94,40 @@
     cb.wait()
     cs.wait()
 
-    def step(k, carry):
+    def split_rows(v):
+        hi, lo = split2(v)
+        return jnp.concatenate([hi, lo, hi], axis=0)
+
+    def split_cols(v):
+        hi, lo = split2(v)
+        return jnp.concatenate([hi, hi, lo], axis=1)
+
+    def step(k, carry, low):
         at = pl.ds(pl.multiple_of(k * NB, NB), NB)
-        u, w = factor_block(m_ref[at, at])
-        new = dot3(w, m_ref[at, :])
-        m_ref[at, :] = new
+        diag = m_ref[at, at]
+        for tile in range(low, n, TILE):
+            right = r_ref[:, tile:tile + TILE]
+            m_ref[low:tile + TILE, tile:tile + TILE] -= jnp.dot(
+                l_ref[low:tile + TILE, :], right, preferred_element_type=jnp.float32
+            )
+            t_ref[:, tile:tile + TILE] -= jnp.dot(x_ref[...], right, preferred_element_type=jnp.float32)
+        u, w = factor_block(diag)
+        new = dot3(w, m_ref[at, low:])
+        m_ref[at, low:] = new
         m_ref[at, at] = u
         x = dot3(t_ref[:, at], w, 1)
-        t_ref[...] = t_ref[...] - dot3(x, new)
+        r_ref[:, low:] = split_rows(new)
+        x_ref[...] = split_cols(x)
 
         @pl.when(k == own)
         def _():
             o_ref[heads:, :] = x
-            line = lax.broadcasted_iota(jnp.int32, (NB, n), 0) + k * NB
-            lane = lax.broadcasted_iota(jnp.int32, (NB, n), 1)
-            mine = jnp.where(lane >= line, m_ref[at, :], 0.0)
+            line = lax.broadcasted_iota(jnp.int32, (NB, n - low), 0) + k * NB
+            lane = lax.broadcasted_iota(jnp.int32, (NB, n - low), 1) + low
+            mine = jnp.where(lane >= line, m_ref[at, low:], 0.0)
             pick = (
-                lax.broadcasted_iota(jnp.int32, (heads, n), 1)
-                == lax.broadcasted_iota(jnp.int32, (heads, n), 0) * groups + grp
+                lax.broadcasted_iota(jnp.int32, (heads, n - low), 1) + low
+                == lax.broadcasted_iota(jnp.int32, (heads, n - low), 0) * groups + grp
             ).astype(jnp.bfloat16)
             hi, lo = split2(mine)
             lo2 = (mine - hi.astype(jnp.float32) - lo.astype(jnp.float32)).astype(jnp.bfloat16)
@@ -117,15 +136,26 @@
                 lax.dot_general(pick, v, nt, preferred_element_type=jnp.float32) for v in (hi, lo, lo2)
             )
 
-        def update(j, c):
-            aj = pl.ds(pl.multiple_of(j * NB, NB), NB)
-            m_ref[aj, :] = m_ref[aj, :] - dot3(jnp.transpose(m_ref[at, aj]), m_ref[at, :])
-            return c
-
-        lax.fori_loop(k + 1, blocks, update, 0)
+        @pl.when(k + 1 < blocks)
+        def _():
+            nxt = pl.ds(pl.multiple_of((k + 1) * NB, NB), NB)
+            m_ref[nxt, low:] -= jnp.dot(
+                split_cols(jnp.transpose(m_ref[at, nxt])), r_ref[:, low:], preferred_element_type=jnp.float32
+            )
+            lane = lax.broadcasted_iota(jnp.int32, (NB, n - low), 1) + low
+            later = jnp.where(lane >= (k + 2) * NB, new, 0.0)
+            l_ref[low:, :] = split_cols(jnp.transpose(later))
+
         return carry
 
-    lax.fori_loop(0, blocks, step, 0)
+    r_ref[...] = jnp.zeros_like(r_ref)
+    l_ref[...] = jnp.zeros_like(l_ref)
+    x_ref[...] = jnp.zeros_like(x_ref)
+    first = 0
+    for last in STOPS:
+        stop = blocks * last // STOPS[-1]
+        lax.fori_loop(first, stop, functools.partial(step, low=first * NB), 0)
+        first = stop
 
 
 def chol_solve(square, rest, own, grp, groups):
@@ -143,7 +173,9 @@
         scratch_shapes=[
             pltpu.VMEM((n, n), jnp.float32),
             pltpu.VMEM(rest.shape, jnp.float32),
-            pltpu.VMEM((NB, NB), jnp.float32),
+            pltpu.VMEM((n, 3 * NB), jnp.bfloat16),
+            pltpu.VMEM((3 * NB, n), jnp.bfloat16),
+            pltpu.VMEM((rest.shape[0], 3 * NB), jnp.bfloat16),
             pltpu.SemaphoreType.DMA((2,)),
         ],
         compiler_params=pltpu.CompilerParams(vmem_limit_bytes=48 * 1024 * 1024),
@@ -154,7 +186,8 @@
 MESH = pl.DeviceIdType.MESH
 
 
-def exchange_kernel(parts_ref, sq_ref, rs_ref, got1, acc, got2, send1, recv1, send2, recv2, sends, arrive):
+def exchange_kernel(feats_ref, prior_ref, ridge_ref, sq_ref, rs_ref, gf, gp, ff, fp, parts_ref, sendf, recvf,
+                    sendp, recvp, got1, acc, got2, send1, recv1, send2, recv2, sends, arrive):
     groups, lanes = sq_ref.shape[:2]
     share, width = sq_ref.shape[2:]
     i = lax.axis_index("row")
@@ -178,6 +211,60 @@
         )
         copy.start()
         return copy
+
+    heads = lanes * share
+    early = []
+    for d, z in enumerate(planes[1:]):
+        early.append(remote(feats_ref.at[:heads], gf.at[i], sendf.at[d], recvf.at[i], (z, c)))
+    for d, z in enumerate(planes[1:]):
+        early.append(remote(prior_ref.at[:heads], gp.at[i], sendp.at[d], recvp.at[i], (z, c)))
+
+    def place(z, value):
+        pick = lax.broadcasted_iota(jnp.int32, (width, heads), 0) == (
+            lax.broadcasted_iota(jnp.int32, (width, heads), 1) * groups + z
+        )
+        return jnp.dot(pick.astype(jnp.bfloat16), value, preferred_element_type=jnp.float32)
+
+    def interleave(own_ref, got, to, sem):
+        to[...] = place(i, own_ref[:heads, :])
+        for z in planes[1:]:
+            pltpu.make_async_copy(got.at[z], got.at[z], sem.at[z]).wait()
+            to[...] += place(z, got[z])
+
+    nt = (((1,), (1,)), ((), ()))
+
+    def dot_nt(a, b):
+        return lax.dot_general(a, b, nt, preferred_element_type=jnp.float32)
+
+    mine = pl.ds(pl.multiple_of(i * heads, heads), heads)
+    interleave(feats_ref, gf, ff, recvf)
+    wide = ff[...]
+    cols = wide.astype(jnp.bfloat16)
+    hi, lo = split2(wide * wide)
+    ones = jnp.ones((8, wide.shape[1]), jnp.bfloat16)
+    col_sq = (dot_nt(ones, hi) + dot_nt(ones, lo))[:1]
+    lead = ff[mine, :]
+    tail = feats_ref[heads:, :]
+    for n, rows in enumerate((lead.astype(jnp.bfloat16), tail)):
+        own = rows.astype(jnp.float32)
+        dist = jnp.sum(own * own, axis=1, keepdims=True) + col_sq - 2.0 * dot_nt(rows, cols)
+        each = rows.shape[0] // lanes
+        for k in range(lanes):
+            parts_ref[k // 2, k % 2, n * share:n * share + each, :width] = dist[k * each:k * each + each]
+    interleave(prior_ref, gp, fp, recvp)
+    cols = fp[...].astype(jnp.bfloat16)
+    line = lax.broadcasted_iota(jnp.int32, (heads, width), 0) + i * heads
+    lane = lax.broadcasted_iota(jnp.int32, (heads, width), 1)
+    first = c * (width // lanes)
+    here = (lane == line) & (lane >= first) & (lane < first + width // lanes)
+    ridge = jnp.where(here, jnp.concatenate([ridge_ref[...]] * lanes, axis=1), 0.0)
+    for n, rows in enumerate((fp[mine, :].astype(jnp.bfloat16), prior_ref[heads:, :])):
+        update = dot_nt(rows, cols)
+        if n == 0:
+            update = update - ridge
+        each = rows.shape[0] // lanes
+        for k in range(lanes):
+            parts_ref[k // 2, k % 2, n * share:n * share + each, width:] = update[k * each:k * each + each]
 
     order = [dg // 2, xn // 2, yn // 2, c // 2]
     pair = [
@@ -256,14 +343,15 @@
         for z in planes:
             await_block(z, col)
         await_rest(col)
-    for copy in pair + across + started:
+    for copy in early + pair + across + started:
         copy.wait_send()
 
 
-def exchange(parts, groups, lanes, share):
-    rows, wide = parts.shape
-    each = rows // lanes
-    width = wide // 2
+def exchange(feats, prior, ridge, groups, lanes, share):
+    width = ridge.shape[0] * lanes
+    each = feats.shape[0] // lanes
+    heads = lanes * share
+    wide = 2 * width
     f32 = jnp.float32
     dma = pltpu.SemaphoreType.DMA
     vmem = pl.BlockSpec(memory_space=pltpu.VMEM)
@@ -273,9 +361,18 @@
             jax.ShapeDtypeStruct((groups, lanes, share, width), f32),
             jax.ShapeDtypeStruct((lanes, each - share, width), f32),
         ),
-        in_specs=[vmem],
+        in_specs=[vmem, vmem, vmem],
         out_specs=(vmem, vmem),
         scratch_shapes=[
+            pltpu.VMEM((groups, heads, feats.shape[1]), feats.dtype),
+            pltpu.VMEM((groups, heads, prior.shape[1]), prior.dtype),
+            pltpu.VMEM((width, feats.shape[1]), f32),
+            pltpu.VMEM((width, prior.shape[1]), f32),
+            pltpu.VMEM((lanes // 2, 2, each, wide), f32),
+            dma((groups - 1,)),
+            dma((groups,)),
+            dma((groups - 1,)),
+            dma((groups,)),
             pltpu.VMEM((4, each, wide), f32),
             pltpu.VMEM((4, each, wide), f32),
             pltpu.VMEM((3, each, wide), f32),
@@ -287,9 +384,9 @@
             dma((groups * lanes + lanes,)),
         ],
         compiler_params=pltpu.CompilerParams(
-            collective_id=1, has_side_effects=True, vmem_limit_bytes=40 * 1024 * 1024
+            collective_id=1, has_side_effects=True, vmem_limit_bytes=56 * 1024 * 1024
         ),
-    )(parts.reshape(lanes // 2, 2, each, wide))
+    )(feats, prior, ridge[None, :])
     return square.reshape(-1, width), rest.reshape(-1, width)
 
 def subject_rows(parts, groups, count):
@@ -303,15 +400,12 @@
     return jnp.concatenate(both, axis=1).reshape(-1, width)
 
 
-def body(feats, prior_factor, ridge):
-    groups = lax.axis_size("row")
-    lanes = lax.axis_size("col")
+def gathered(feats, prior_factor, ridge, groups, lanes, share):
     row_pos = lax.axis_index("row")
     col_pos = lax.axis_index("col")
     cols_here = ridge.shape[0]
     total_cols = cols_here * lanes
-    leading = total_cols // groups
-    share = leading // lanes
+    leading = share * lanes
     col_feats, col_prior = (
         lax.all_gather(feats[:leading], "row", axis=0, tiled=True),
         lax.all_gather(prior_factor[:leading], "row", axis=0, tiled=True),
@@ -339,17 +433,24 @@
     )
     update = jnp.dot(rows_prior, col_prior.T, preferred_element_type=jnp.float32)
     update = update - jnp.where(subject == column, own_ridge[None, :], 0.0)
-    parts = jnp.concatenate([dist, update], axis=1)
-    if (groups, lanes) == (4, 8):
-        square, rest = exchange(parts, groups, lanes, share)
-    else:
-        sums = lax.psum_scatter(
-            parts, "col", scatter_dimension=0, tiled=True
-        )
-        system = jnp.exp(-sums[:, :total_cols] / EDGES) - sums[:, total_cols:]
-        square = lax.all_gather(system[:share], ("row", "col"), axis=0, tiled=True)
-        rest = lax.all_gather(system[share:], "col", axis=0, tiled=True)
-    out = chol_solve(square, rest, col_start // NB, row_pos, groups)
+    sums = lax.psum_scatter(
+        jnp.concatenate([dist, update], axis=1), "col", scatter_dimension=0, tiled=True
+    )
+    system = jnp.exp(-sums[:, :total_cols] / EDGES) - sums[:, total_cols:]
+    square = lax.all_gather(system[:share], ("row", "col"), axis=0, tiled=True)
+    rest = lax.all_gather(system[share:], "col", axis=0, tiled=True)
+    return square, rest
+
+
+def body(feats, prior_factor, ridge):
+    groups = lax.axis_size("row")
+    lanes = lax.axis_size("col")
+    cols_here = ridge.shape[0]
+    share = cols_here // groups
+    col_start = lax.axis_index("col") * cols_here
+    form = exchange if (groups, lanes) == (4, 8) else gathered
+    square, rest = form(feats, prior_factor, ridge, groups, lanes, share)
+    out = chol_solve(square, rest, col_start // NB, lax.axis_index("row"), groups)
     if cols_here < NB:
         out = lax.dynamic_slice_in_dim(out, col_start % NB, cols_here, 1)
     return out

time: 172 us -> 142 us (0.83)
  the two profiles are of different devices: /device:TPU:11 before, /device:TPU:0 now
where the time goes in v3:
time: 142 us; the launch traced here: 141 us
  Pallas kernels  137 us (96%)
  local copies, waits for them, and re-layouts  3.41 us (2%)
    pallas_call x1, Pallas kernels, exchange(): pl.pallas_call(exchange_kernel, out_shape=(jax.ShapeDtypeStruct((groups,...  101 us
    pallas_call x1, Pallas kernels, chol_solve(): pl.pallas_call(chol_kernel, out_shape=jax.ShapeDtypeStruct((n // groups +...  36.9 us
    unnamed x4, local copies, waits for them, and re-layouts  3.41 us

profile of v3, /device:TPU:0, one launch (start us, length us, event | category | flops | bytes accessed | tf_op | source)
XLA Modules:
  0.0 140.9 jit_solution(6736550631768188419)
XLA Ops:
  0.0 0.1 pad_add_fusion.col_ref
  0.1 100.6 %shard_map.37 = (f32[4,8,32,1024]{3,2,1,0:T(8,128)}, f32[8,32,1024]{2,1,0:T(8,128)}) custom-call(bf16[512,512]{1,0:T(8,128)(2,1)} %feats_ref.1, bf16[512,256]{1,0:T(8,128)(2,1)} %prior_ref.1, f32[1,128]{1,0:T(1,128)} %bitcast.7), custom_call_target="tpu_custom_call" | custom-call | tf_op jit(solution)/shard_map/pallas_call | solution.py:358
  100.6 0.0 copy-start
  100.7 2.2 %copy-done = f32[4,8,32,1024]{3,2,1,0:T(8,128)S(1)} copy-done((f32[4,8,32,1024]{3,2,1,0:T(8,128)S(1)}, f32[4,8,32,1024]{3,2,1,0:T(8,128)}, u32[]{:S(2)}) %copy-start) | copy-done | bytes 4194328
  102.8 0.0 copy-start.1
  102.8 1.2 copy-done.1
  104.1 36.9 %shard_map.38 = f32[512,128]{1,0:T(8,128)} custom-call(s32[6]{0:T(128)S(1)} %pad_add_fusion.col_ref, f32[1024,1024]{1,0:T(8,128)S(1)} %bitcast.5, f32[256,1024]{1,0:T(8,128)S(1)} %bitcast.6), custom_call_target="tpu_custom_call" | custom-call | tf_op jit(solution)/shard_map/pallas_call | solution.py:164
  (1 shorter events, 0.0 us)
Async XLA Ops:
  100.6 2.2 %copy-start = (f32[4,8,32,1024]{3,2,1,0:T(8,128)S(1)}, f32[4,8,32,1024]{3,2,1,0:T(8,128)}, u32[]{:S(2)}) copy-start(f32[4,8,32,1024]{3,2,1,0:T(8,128)} %get-tuple-element.7) | copy-start | bytes 12582916
  102.8 1.2 copy-start.1

commit v4 on v3

--- a/solution.py
+++ b/solution.py
@@ -251,6 +251,28 @@
         each = rows.shape[0] // lanes
         for k in range(lanes):
             parts_ref[k // 2, k % 2, n * share:n * share + each, :width] = dist[k * each:k * each + each]
+    order = [dg // 2, xn // 2, yn // 2, c // 2]
+    pair = []
+    across = []
+
+    def add_over_pair(h):
+        half = pl.ds(h * width, width)
+        begun = [
+            remote(parts_ref.at[q, 1 - core, :, half], got1.at[4 * h + n], send1.at[4 * h + n],
+                   recv1.at[4 * h + n], (i, sib))
+            for n, q in enumerate(order)
+        ]
+        pair.extend(begun)
+        for n, q in enumerate(order):
+            begun[n].wait_recv()
+            acc[4 * h + n] = parts_ref[q, core, :, half] + got1[4 * h + n]
+            if n < 3:
+                across.append(
+                    remote(acc.at[4 * h + n], got2.at[3 * h + n], send2.at[3 * h + n],
+                           recv2.at[3 * h + n], (i, (dg, xn, yn)[n]))
+                )
+
+    add_over_pair(0)
     interleave(prior_ref, gp, fp, recvp)
     cols = fp[...].astype(jnp.bfloat16)
     line = lax.broadcasted_iota(jnp.int32, (heads, width), 0) + i * heads
@@ -266,23 +288,11 @@
         for k in range(lanes):
             parts_ref[k // 2, k % 2, n * share:n * share + each, width:] = update[k * each:k * each + each]
 
-    order = [dg // 2, xn // 2, yn // 2, c // 2]
-    pair = [
-        remote(parts_ref.at[q, 1 - core], got1.at[n], send1.at[n], recv1.at[n], (i, sib))
-        for n, q in enumerate(order)
-    ]
-    across = []
-    for n, q in enumerate(order):
-        pair[n].wait_recv()
-        acc[n] = parts_ref[q, core] + got1[n]
-        if n < 3:
-            across.append(
-                remote(acc.at[n], got2.at[n], send2.at[n], recv2.at[n], (i, (dg, xn, yn)[n]))
-            )
+    add_over_pair(1)
     for copy in across:
         copy.wait_recv()
-    total = acc[3] + got2[0] + got2[1] + got2[2]
-    system = jnp.exp(-total[:, :width] / EDGES) - total[:, width:]
+    dist, update = [acc[4 * h + 3] + got2[3 * h] + got2[3 * h + 1] + got2[3 * h + 2] for h in range(2)]
+    system = jnp.exp(-dist / EDGES) - update
     sq_ref[i, c] = system[:share]
     rs_ref[c] = system[share:]
 
@@ -373,13 +383,13 @@
             dma((groups,)),
             dma((groups - 1,)),
             dma((groups,)),
-            pltpu.VMEM((4, each, wide), f32),
-            pltpu.VMEM((4, each, wide), f32),
-            pltpu.VMEM((3, each, wide), f32),
-            dma((4,)),
-            dma((4,)),
-            dma((3,)),
-            dma((3,)),
+            pltpu.VMEM((8, each, width), f32),
+            pltpu.VMEM((8, each, width), f32),
+            pltpu.VMEM((6, each, width), f32),
+            dma((8,)),
+            dma((8,)),
+            dma((6,)),
+            dma((6,)),
             dma((64,)),
             dma((groups * lanes + lanes,)),
         ],

time: 142 us -> 137 us (0.965)
  Pallas kernels: 137 us -> 132 us
    pallas_call x1, Pallas kernels: 101 us -> 95.1 us  [exchange(): pl.pallas_call(exchange_kernel, out_shape=(jax.ShapeDtypeStruct((groups,...]
where the time goes in v4:
time: 137 us; the launch traced here: 135 us
  Pallas kernels  132 us (96%)
  local copies, waits for them, and re-layouts  3.41 us (2%)
    pallas_call x1, Pallas kernels, exchange(): pl.pallas_call(exchange_kernel, out_shape=(jax.ShapeDtypeStruct((groups,...  95.1 us
    pallas_call x1, Pallas kernels, chol_solve(): pl.pallas_call(chol_kernel, out_shape=jax.ShapeDtypeStruct((n // groups +...  36.9 us
    unnamed x4, local copies, waits for them, and re-layouts  3.41 us

profile of v4, /device:TPU:0, one launch (start us, length us, event | category | flops | bytes accessed | tf_op | source)
XLA Modules:
  0.0 135.5 jit_solution(10939872890277800594)
XLA Ops:
  0.0 0.1 pad_add_fusion.col_ref
  0.1 95.1 %shard_map.37 = (f32[4,8,32,1024]{3,2,1,0:T(8,128)}, f32[8,32,1024]{2,1,0:T(8,128)}) custom-call(bf16[512,512]{1,0:T(8,128)(2,1)} %feats_ref.1, bf16[512,256]{1,0:T(8,128)(2,1)} %prior_ref.1, f32[1,128]{1,0:T(1,128)} %bitcast.7), custom_call_target="tpu_custom_call" | custom-call | tf_op jit(solution)/shard_map/pallas_call | solution.py:368
  95.2 0.0 copy-start
  95.2 2.2 %copy-done = f32[4,8,32,1024]{3,2,1,0:T(8,128)S(1)} copy-done((f32[4,8,32,1024]{3,2,1,0:T(8,128)S(1)}, f32[4,8,32,1024]{3,2,1,0:T(8,128)}, u32[]{:S(2)}) %copy-start) | copy-done | bytes 4194328
  97.4 0.0 copy-start.1
  97.4 1.2 copy-done.1
  98.6 36.9 %shard_map.38 = f32[512,128]{1,0:T(8,128)} custom-call(s32[6]{0:T(128)S(1)} %pad_add_fusion.col_ref, f32[1024,1024]{1,0:T(8,128)S(1)} %bitcast.5, f32[256,1024]{1,0:T(8,128)S(1)} %bitcast.6), custom_call_target="tpu_custom_call" | custom-call | tf_op jit(solution)/shard_map/pallas_call | solution.py:164
  (1 shorter events, 0.0 us)
Async XLA Ops:
  95.2 2.2 %copy-start = (f32[4,8,32,1024]{3,2,1,0:T(8,128)S(1)}, f32[4,8,32,1024]{3,2,1,0:T(8,128)}, u32[]{:S(2)}) copy-start(f32[4,8,32,1024]{3,2,1,0:T(8,128)} %get-tuple-element.7) | copy-start | bytes 12582916
  97.4 1.2 copy-start.1
